TPU v7x, 512 devices: a whole 4x8x8 slice. The times are simulated.
512 devices in a mesh: req: 8 (over z), head: 8 (over y_lo, core), ffn: 8 (over y_hi, x).
Axes of the slice: x: 4, y: 8 (y_hi: 2, y_lo: 4; y = y_hi * 4 + y_lo), z: 8, core: 2. Of those that a mesh axis runs over, the one named last changes fastest.
Arguments:
- queries: bfloat16 [512, 16384], P(('req', 'ffn'), 'head'), may hold values from -11 to 11
- key_cache: bfloat16 [512, 256, 1024], P(('req', 'ffn'), None, 'head'), may hold values from -4 to 4
- value_cache: bfloat16 [512, 256, 1024], P(('req', 'ffn'), None, 'head'), may hold values from -5 to 5
- new_key: bfloat16 [512, 1024], P(('req', 'ffn'), 'head'), may hold values from -5 to 5
- new_value: bfloat16 [512, 1024], P(('req', 'ffn'), 'head'), may hold values from -5 to 5
- lengths: int32 [512], P(('req', 'ffn')), may hold values from 2 to 256, as said below
- residual: bfloat16 [512, 16384], P(('req', 'ffn'), 'head'), may hold values from -40 to 40
- norm_gain: bfloat16 [16384], P('head'), may hold values from 0.099609375 to 1.8984375
- w_gate: bfloat16 [16384, 32768], P('head', ('req', 'ffn')), may hold values from -0.046875 to 0.046875
- w_down: bfloat16 [32768, 16384], P(('req', 'ffn'), 'head'), may hold values from -0.03125 to 0.03125
Outputs:
- result: bfloat16 [512, 16384], P(('req', 'ffn'), 'head')
Inputs may be any that keep to these rules, and one draw needn't show every extreme that they name: `lengths`: every request has at least two cached tokens; some request fills all 256 slots.
All inputs are finite; a program needn't handle non-finite values.
Results may differ from a plain program's by a relative error of at most 0.0075.
Values may be sent and summed in bfloat16 or wider, within the bound.
A program may use at most 64 MiB of HBM per device.

v0:
```python
import jax
import jax.numpy as jnp
from jax import lax
from jax.sharding import PartitionSpec as P

D = 16384
QH = 128
KVH = 8
HD = 128
CACHE = 256


EPSILON = 1e-05


def attend(queries, key_cache, value_cache, new_key, new_value, lengths):
    row_count = queries.shape[0]
    kv_local = new_key.shape[1] // HD
    per_group = QH // KVH
    score_scale = HD ** (-0.5)
    query_heads = queries.reshape(row_count, kv_local, per_group, HD)
    key_block = key_cache.reshape(row_count, CACHE, kv_local, HD)
    value_block = value_cache.reshape(row_count, CACHE, kv_local, HD)
    fresh_key = new_key.reshape(row_count, kv_local, HD)
    fresh_value = new_value.reshape(row_count, kv_local, HD)
    scores = (
        jnp.einsum("rkgd,rlkd->rkgl", query_heads, key_block, preferred_element_type=jnp.float32)
        * score_scale
    )
    self_score = (
        jnp.einsum("rkgd,rkd->rkg", query_heads, fresh_key, preferred_element_type=jnp.float32)
        * score_scale
    )
    visible = jnp.arange(CACHE, dtype=jnp.int32)[None, None, None, :] < lengths[:, None, None, None]
    maximum = jnp.maximum(jnp.max(jnp.where(visible, scores, -1e30), axis=-1), self_score)
    raised = jnp.where(visible, jnp.exp(scores - maximum[..., None]), 0.0)
    self_raised = jnp.exp(self_score - maximum)
    totals = jnp.sum(raised, axis=-1) + self_raised
    weights = (raised / totals[..., None]).astype(jnp.bfloat16)
    self_weight = (self_raised / totals).astype(jnp.bfloat16)
    blended = jnp.einsum(
        "rkgl,rlkd->rkgd", weights, value_block, preferred_element_type=jnp.float32
    )
    blended = (
        blended
        + self_weight.astype(jnp.float32)[..., None]
        * fresh_value.astype(jnp.float32)[:, :, None, :]
    )
    return blended.reshape(row_count, kv_local * per_group * HD).astype(jnp.bfloat16)


def per_device(
    queries,
    key_cache,
    value_cache,
    new_key,
    new_value,
    lengths,
    residual,
    norm_gain,
    w_gate,
    w_down,
):
    attended = attend(queries, key_cache, value_cache, new_key, new_value, lengths)
    stream = (residual.astype(jnp.float32) + attended.astype(jnp.float32)).astype(jnp.bfloat16)
    stream_wide = stream.astype(jnp.float32)
    squares = lax.psum(jnp.sum(stream_wide * stream_wide, axis=1), "head")
    inverse = lax.rsqrt(squares / D + EPSILON)
    normed = (stream_wide * inverse[:, None] * norm_gain.astype(jnp.float32)[None, :]).astype(
        jnp.bfloat16
    )
    partial_value = jnp.dot(
        lax.all_gather(normed, ("req", "ffn"), axis=0, tiled=True),
        w_gate,
        preferred_element_type=jnp.float32,
    )
    gate_pre = lax.psum(partial_value, "head")
    hidden = jax.nn.silu(gate_pre).astype(jnp.bfloat16)
    ffn_out = lax.psum_scatter(
        jnp.dot(hidden, w_down, preferred_element_type=jnp.float32),
        ("req", "ffn"),
        scatter_dimension=0,
        tiled=True,
    )
    return (stream_wide + ffn_out).astype(jnp.bfloat16)


def solution(mesh):
    return jax.shard_map(
        per_device,
        mesh=mesh,
        in_specs=(
            P(("req", "ffn"), "head"),
            P(("req", "ffn"), None, "head"),
            P(("req", "ffn"), None, "head"),
            P(("req", "ffn"), "head"),
            P(("req", "ffn"), "head"),
            P(("req", "ffn")),
            P(("req", "ffn"), "head"),
            P("head"),
            P("head", ("req", "ffn")),
            P(("req", "ffn"), "head"),
        ),
        out_specs=P(("req", "ffn"), "head"),
        check_vma=False,
    )
```

profile of v0, /device:TPU:8, one launch (start us, length us, event | category | flops | bytes accessed | tf_op | source)
XLA Modules:
  0.0 709.4 jit_solution(12097819844886372169)
XLA Ops:
  6.5 0.0 copy-start
  6.5 0.0 all-gather.2.cloned.1.call-start
  6.5 0.9 iota_compare_fusion
  7.4 0.7 convert_element_type.51
  8.1 0.7 convert_element_type.57
  8.8 0.9 fusion.15
  9.7 1.4 select_reduce_fusion
  11.1 0.2 fusion.5
  11.3 1.3 fusion.2
  12.6 0.9 fusion.6
  13.5 15.4 %psum.14 = f32[8]{0:T(128)S(1)} all-reduce(f32[8]{0:T(128)S(1)} %get-tuple-element.5), channel_id=1, replica_groups=mesh['req'=8,'head'=8,'ffn'=8] {'head'}, use_global_device_ids=true, to_apply=%region_3.4 | all-reduce | flops 8 | bytes 64 | tf_op jit(solution)/shard_map/psum | solution.py:67
  28.8 0.7 fusion.8
  29.5 0.0 all-gather.2.cloned.1.call-update
  29.6 0.0 all-reduce.2.cloned.1.call-start
  29.6 138.6 %all-gather.2.cloned.1.call-done = bf16[512,2048]{1,0:T(8,128)(2,1)} async-done(((bf16[8,2048]{1,0:T(8,128)(2,1)}), bf16[512,2048]{1,0:T(8,128)(2,1)}) %all-gather.2.cloned.1.call-update) | async-done | bytes 2097168 | tf_op jit(solution)/shard_map/all_gather | solution.py:73
  168.3 4.5 fusion.24
  172.7 0.0 all-reduce.2.cloned.1.call-update
  172.7 0.0 reduce-scatter.2.cloned.1.call-start
  172.8 71.0 %all-reduce.2.cloned.1.call-done = f32[512,512]{1,0:T(8,128)} async-done(((f32[512,512]{1,0:T(8,128)}), f32[512,512]{1,0:T(8,128)}) %all-reduce.2.cloned.1.call-update) | async-done | bytes 1048592 | tf_op jit(solution)/shard_map/psum | solution.py:77
  243.7 0.0 copy-done
  243.7 4.4 fusion.3
  248.2 0.0 reduce-scatter.2.cloned.1.call-update
  248.2 453.2 %reduce-scatter.2.cloned.1.call-done = f32[8,2048]{1,0:T(8,128)} async-done(((f32[512,2048]{1,0:T(8,128)}), f32[8,2048]{1,0:T(8,128)}) %reduce-scatter.2.cloned.1.call-update) | async-done | bytes 65552 | tf_op jit(solution)/shard_map/reduce_scatter | solution.py:79
  701.4 1.5 fusion.9
  (3 shorter events, 0.0 us)
Async XLA Ops:
  6.5 237.2 %copy-start = (bf16[512,2048]{1,0:T(8,128)(2,1)S(1)}, bf16[512,2048]{1,0:T(8,128)(2,1)}, u32[]{:S(2)}) copy-start(bf16[512,2048]{1,0:T(8,128)(2,1)} %param.19) | copy-start | bytes 6291460
  6.5 161.7 %all-gather.2.cloned.1.call-start = ((), (), s32[]{:S(2)}) async-start(), calls=%async_computation.1 | async-start | bytes 2129920 | tf_op jit(solution)/shard_map/all_gather | solution.py:73
  29.6 214.2 %all-reduce.2.cloned.1.call-start = ((), (), s32[]{:S(2)}) async-start(), calls=%async_computation.2 | async-start | bytes 2097152 | tf_op jit(solution)/shard_map/psum | solution.py:77
  172.7 528.7 %reduce-scatter.2.cloned.1.call-start = ((), (), s32[]{:S(2)}) async-start(), calls=%async_computation.3 | async-start | bytes 4259840 | tf_op jit(solution)/shard_map/reduce_scatter | solution.py:79
Sparse Core Ops, SparseCore 0:
  29.7 138.5 all-gather.1
  172.9 70.8 all-reduce.1
  248.3 453.0 reduce-scatter.1
where the time goes:
time: 710 us; the launch traced here: 709 us
  waiting for transfers between devices  663 us (93%)
  blocking collectives  15.4 us (2%)
  between operations  13.1 us (2%)
  matrix products  12.5 us (2%)
    reduce_scatter x1, waiting for transfers between devices, per_device(): lax.psum_scatter(jnp.dot(hidden, w_down, preferred_element_type=jnp.float...  453 us
    all_gather x1, waiting for transfers between devices, per_device(): lax.all_gather(normed, ('req', 'ffn'), axis=0, tiled=True)  139 us
    psum x1, waiting for transfers between devices, per_device(): gate_pre = lax.psum(partial_value, 'head')  71 us
    psum x1, blocking collectives, per_device(): squares = lax.psum(jnp.sum(stream_wide * stream_wide, axis=1), 'head')  15.4 us
  transfers between devices with their start and end apart: 3, of which 3 were waited for; matrix products, arithmetic and copies ran while one was open for 0% of the time, Pallas kernels for 0%

commit v1 on v0

v1 whole, which is shorter than its diff:
```python
import jax
import jax.numpy as jnp
from jax import lax
from jax.experimental import pallas as pl
from jax.experimental.pallas import tpu as pltpu
from jax.sharding import PartitionSpec as P

D = 16384
EPSILON = 1e-05
NZ = 8
NX = 4
NY = 4
ROWS = 8
HEADS = 16
HD = 128
CACHE = 256
WIDTH = 2048
HALF = WIDTH // 2
HIDDEN = 512
QUARTER = HIDDEN // NY
MESH = pl.DeviceIdType.MESH
F32 = jnp.float32
BF16 = jnp.bfloat16

GROUPS = (
    (("E", 0), ("O", 0)),
    (("E", 1), ("E", 7)),
    (("E", 2), ("E", 6), ("O", 1), ("O", 3)),
    (("E", 3), ("E", 5)),
    (("E", 4), ("O", 2)),
)
FLOW = {"E": 0, "O": 1}
BLOCKS = {"E": NX, "O": NZ}


def group_rows(group):
    return sum(BLOCKS[kind] * ROWS for kind, _ in group)


def offset_of(g):
    return sum(group_rows(group) for group in GROUPS[:g]) // 2


RING_ORDER = (("p", 0), ("m", 1), ("p", 1), ("m", 0))


def hops_of(n, direction, half):
    far = 0 if direction == "p" else 1
    return n // 2 if half == far else n // 2 - 1


def fold(wide):
    return jnp.concatenate([wide[:, :HALF], wide[:, HALF:]], axis=0)


def unfold(folded):
    return jnp.concatenate([folded[:ROWS], folded[ROWS:]], axis=1)


def kernel(
    q_ref,
    k_hbm,
    v_hbm,
    nk_ref,
    nv_ref,
    len_ref,
    res_ref,
    gain_ref,
    wg_hbm,
    wd_hbm,
    out_ref,
    k_ref,
    v_ref,
    wg_ref,
    wd_ref,
    sq_ref,
    ysend,
    yrecv,
    stream_ref,
    x_ref,
    xu_ref,
    p_ref,
    s1_send,
    s1_recv,
    s2_own,
    s2_send,
    s2_recv,
    hid_ref,
    d_ref,
    re_ref,
    ro_ref,
    fe_ref,
    fo_ref,
    fsum_ref,
    zsend,
    zrecv,
    load_sem,
    send_sem,
    recv_sem,
):
    z = lax.axis_index("req")
    head = lax.axis_index("head")
    ffn = lax.axis_index("ffn")
    yq, core = head // 2, head % 2
    yh, x = ffn // NX, ffn % NX

    def along_z(step):
        return {"req": (z + step) % NZ}

    def along_x(step):
        return {"ffn": yh * NX + (x + step) % NX}

    def along_y(step):
        return {"head": ((yq + step) % NY) * 2 + core}

    other_core = {"head": yq * 2 + 1 - core}
    other_half = {"ffn": (1 - yh) * NX + x}

    def same_rows(dh, dk):
        return {"ffn": ((yh + dh) % 2) * NX + x, "head": (head + dk) % 8}

    loads = []
    for i, (src, dst) in enumerate(
        ((k_hbm, k_ref), (v_hbm, v_ref), (wg_hbm, wg_ref), (wd_hbm, wd_ref))
    ):
        copy = pltpu.make_async_copy(src, dst, load_sem.at[i])
        copy.start()
        loads.append(copy)

    peers = [same_rows(dh, dk) for dh in range(2) for dk in range(8) if dh or dk]
    peers += [along_x(k) for k in range(1, NX)]
    peers += [along_z(k) for k in range(1, NZ)]
    barrier = pltpu.get_barrier_semaphore()
    for peer in peers:
        pl.semaphore_signal(barrier, inc=1, device_id=peer, device_id_type=MESH)

    copies = []

    def send(src, dst, device):
        i = len(copies)
        copy = pltpu.make_async_remote_copy(
            src_ref=src,
            dst_ref=dst,
            send_sem=send_sem.at[i],
            recv_sem=recv_sem.at[i],
            device_id=device,
            device_id_type=MESH,
        )
        copy.start()
        copies.append(copy)
        return copy

    q = q_ref[...].astype(F32)
    q_all = jnp.concatenate([q[:, HD * j : HD * (j + 1)] for j in range(HEADS)], axis=0)
    request = lax.broadcasted_iota(jnp.int32, (HEADS * ROWS, 1), 0) % ROWS
    limit = jnp.zeros((HEADS * ROWS, 1), jnp.int32)
    for r in range(ROWS):
        limit = jnp.where(request == r, len_ref[r], limit)
    scale = HD ** (-0.5)
    new_key = jnp.concatenate([nk_ref[...].astype(F32)] * HEADS, axis=0)
    new_value = jnp.concatenate([nv_ref[...].astype(F32)] * HEADS, axis=0)
    self_score = jnp.sum(q_all * new_key, axis=1, keepdims=True) * scale
    loads[0].wait()
    scores = jnp.zeros((HEADS * ROWS, CACHE), F32)
    for r in range(ROWS):
        scores += lax.dot_general(
            jnp.where(request == r, q_all, 0.0).astype(BF16),
            k_ref[r],
            (((1,), (1,)), ((), ())),
            preferred_element_type=F32,
        )
    scores = scores * scale
    visible = lax.broadcasted_iota(jnp.int32, scores.shape, 1) < limit
    maximum = jnp.maximum(
        jnp.max(jnp.where(visible, scores, -1e30), axis=1, keepdims=True), self_score
    )
    raised = jnp.where(visible, jnp.exp(scores - maximum), 0.0)
    self_raised = jnp.exp(self_score - maximum)
    totals = jnp.sum(raised, axis=1, keepdims=True) + self_raised
    weights = raised / totals
    self_weight = (self_raised / totals).astype(BF16).astype(F32)
    loads[1].wait()
    blended = self_weight * new_value
    for r in range(ROWS):
        blended += jnp.dot(
            jnp.where(request == r, weights, 0.0).astype(BF16),
            v_ref[r],
            preferred_element_type=F32,
        )
    attended = jnp.concatenate(
        [blended[ROWS * j : ROWS * (j + 1)] for j in range(HEADS)], axis=1
    ).astype(BF16)
    stream = (res_ref[...].astype(F32) + attended.astype(F32)).astype(BF16).astype(F32)
    stream_ref[...] = stream
    squares = stream * stream
    part = squares[:, :HD]
    for j in range(1, HEADS):
        part += squares[:, HD * j : HD * (j + 1)]
    sq_ref[0, 0] = part
    ysend[...] = fold(stream).astype(BF16)

    pl.semaphore_wait(barrier, len(peers))

    ycopy = send(ysend, yrecv, other_half)
    sq_copies = []
    for dh in range(2):
        for dk in range(8):
            if dh or dk:
                sq_copies.append(
                    send(sq_ref.at[0, 0], sq_ref.at[dh, (8 - dk) % 8], same_rows(dh, dk))
                )
    gain = gain_ref[...].astype(F32)

    def normed(rows, dh):
        total = sq_ref[dh, 0]
        for dk in range(1, 8):
            total += sq_ref[dh, dk]
        inverse = lax.rsqrt(jnp.sum(total, axis=1, keepdims=True) / D + EPSILON)
        return fold(rows * inverse * gain).astype(BF16)

    for copy in sq_copies:
        copy.wait_recv()
    x_ref[yh, 0] = normed(stream, 0)
    ycopy.wait_recv()
    x_ref[1 - yh, 0] = normed(unfold(yrecv[...].astype(F32)), 1)

    o_first = []
    for k in (4, 3, 5, 2, 6, 1, 7):
        o_first.append(send(x_ref.at[1, 0], x_ref.at[1, NZ - k], along_z(k)))
    e_first = []
    for k in (2, 1, 3):
        e_first.append(send(x_ref.at[0, 0], x_ref.at[0, NX - k], along_x(k)))

    rings = {"E": (NZ, along_z), "O": (NX, along_x)}

    def chunk(ref, kind, slot, half):
        blocks = BLOCKS[kind] // 2
        return ref.at[FLOW[kind], pl.ds(slot * BLOCKS[kind] + half * blocks, blocks)]

    arriving = {}

    def gather_hop(kind, s):
        n, along = rings[kind]
        for direction, half in RING_ORDER:
            if (kind, direction, half, s - 1) in arriving:
                arriving[kind, direction, half, s - 1].wait_recv()
            if s >= hops_of(n, direction, half):
                continue
            step = 1 if direction == "p" else -1
            arriving[kind, direction, half, s] = send(
                chunk(x_ref, kind, (-step * s) % n, half),
                chunk(x_ref, kind, (-step * (s + 1)) % n, half),
                along(step),
            )

    step_copies = {}

    def gate(g):
        row = 0
        for kind, slot in GROUPS[g]:
            n = BLOCKS[kind]
            folded = x_ref[FLOW[kind], slot * n : (slot + 1) * n].astype(F32)
            low = folded[:, :ROWS].reshape(n * ROWS, HALF).astype(BF16)
            high = folded[:, ROWS:].reshape(n * ROWS, HALF).astype(BF16)
            xu_ref[row : row + n * ROWS, :HALF] = low
            xu_ref[row : row + n * ROWS, HALF:] = high
            row += n * ROWS
        m, o = row // 2, offset_of(g)
        value = jnp.dot(xu_ref[:row, :], wg_ref[...], preferred_element_type=F32)
        p_ref[0, o : o + m] = value[:m]
        p_ref[1, o : o + m] = value[m:]
        s1_send[o : o + m] = p_ref[1 - core, o : o + m].astype(BF16)
        step_copies[1, g] = [
            send(s1_send.at[pl.ds(o, m)], s1_recv.at[pl.ds(o, m)], other_core)
        ]

    def reduce_y(g):
        m, o = group_rows(GROUPS[g]) // 2, offset_of(g)
        for copy in step_copies[1, g]:
            copy.wait_recv()
        value = p_ref[core, o : o + m] + s1_recv[o : o + m].astype(F32)
        for j in range(NY):
            piece = value[:, QUARTER * j : QUARTER * (j + 1)]
            s2_own[j, o : o + m] = piece
            s2_send[j, o : o + m] = piece.astype(BF16)
        step_copies[2, g] = [
            send(
                s2_send.at[(yq + k) % NY, pl.ds(o, m)],
                s2_recv.at[k - 1, pl.ds(o, m)],
                along_y(k),
            )
            for k in (2, 1, 3)
        ]

    def activate(g):
        m, o = group_rows(GROUPS[g]) // 2, offset_of(g)
        for copy in step_copies[2, g]:
            copy.wait_recv()
        value = s2_own[yq, o : o + m]
        for k in range(NY - 1):
            value += s2_recv[k, o : o + m].astype(F32)
        hid_ref[core, yq, o : o + m] = (value / (1.0 + jnp.exp(-value))).astype(BF16)
        piece = hid_ref.at[core, yq, pl.ds(o, m)]
        step_copies[3, g] = [send(piece, piece, along_y(k)) for k in (2, 1, 3)]

    def share_core(g):
        m, o = group_rows(GROUPS[g]) // 2, offset_of(g)
        for copy in step_copies[3, g]:
            copy.wait_recv()
        piece = hid_ref.at[core, :, pl.ds(o, m)]
        step_copies[4, g] = [send(piece, piece, other_core)]

    def down(g):
        m, o = group_rows(GROUPS[g]) // 2, offset_of(g)
        for copy in step_copies[4, g]:
            copy.wait_recv()
        hidden = jnp.concatenate(
            [
                jnp.concatenate([hid_ref[c, j, o : o + m] for j in range(NY)], axis=1)
                for c in range(2)
            ],
            axis=0,
        )
        tile = 256
        for t in range(HALF // tile):
            columns = pl.ds(t * tile, tile)
            low = jnp.dot(
                hidden, wd_ref[:, t * tile : (t + 1) * tile], preferred_element_type=F32
            ).reshape(2 * m // ROWS, ROWS, tile)
            high = jnp.dot(
                hidden,
                wd_ref[:, HALF + t * tile : HALF + (t + 1) * tile],
                preferred_element_type=F32,
            ).reshape(2 * m // ROWS, ROWS, tile)
            both = jnp.concatenate([low, high], axis=1).astype(BF16)
            row = 0
            for kind, slot in GROUPS[g]:
                n = BLOCKS[kind]
                d_ref[FLOW[kind], slot * n : (slot + 1) * n, :, columns] = both[row : row + n]
                row += n

    for copy in e_first:
        copy.wait_recv()
    gather_hop("E", 0)
    for copy in o_first:
        copy.wait_recv()
    gather_hop("O", 0)
    loads[2].wait()
    gate(0)
    gather_hop("E", 1)
    gate(1)
    reduce_y(0)
    gather_hop("O", 1)
    gather_hop("E", 2)
    activate(0)
    gate(2)
    reduce_y(1)
    gather_hop("E", 3)
    activate(1)
    share_core(0)
    gate(3)
    reduce_y(2)
    activate(2)
    share_core(1)
    gather_hop("E", 4)
    gather_hop("O", 2)
    gate(4)
    reduce_y(3)
    loads[3].wait()
    down(0)
    reduce_y(4)
    activate(3)
    share_core(2)
    down(1)
    activate(4)
    share_core(3)
    down(2)
    share_core(4)
    down(3)
    down(4)

    recv_at = {"E": {}, "O": {}}
    for kind in ("E", "O"):
        n, _ = rings[kind]
        count = 0
        for direction, half in RING_ORDER:
            for s in range(hops_of(n, direction, half)):
                recv_at[kind][direction, half, s] = count
                count += 1
    recv_refs = {"E": re_ref, "O": ro_ref}
    sums = {}

    def scatter_hop(kind, s):
        n, along = rings[kind]
        landing = recv_refs[kind]
        blocks = BLOCKS[kind] // 2
        for direction, half in RING_ORDER:
            hops, t = hops_of(n, direction, half), s
            if t >= hops:
                continue
            step = 1 if direction == "p" else -1
            slot = (step * (hops - t)) % n
            if t > 0:
                sums[kind, direction, half, t - 1].wait_recv()
                first = slot * BLOCKS[kind] + half * blocks
                own = d_ref[FLOW[kind], first : first + blocks].astype(F32)
                came = landing[recv_at[kind][direction, half, t - 1]].astype(F32)
                d_ref[FLOW[kind], first : first + blocks] = (own + came).astype(BF16)
            sums[kind, direction, half, t] = send(
                chunk(d_ref, kind, slot, half),
                landing.at[recv_at[kind][direction, half, t]],
                along(step),
            )

    def scatter_end(kind):
        n, _ = rings[kind]
        blocks = BLOCKS[kind] // 2
        for half in range(2):
            value = d_ref[FLOW[kind], half * blocks : (half + 1) * blocks].astype(F32)
            for direction in ("p", "m"):
                last = hops_of(n, direction, half) - 1
                sums[kind, direction, half, last].wait_recv()
                value += recv_refs[kind][recv_at[kind][direction, half, last]].astype(F32)
            d_ref[FLOW[kind], half * blocks : (half + 1) * blocks] = value.astype(BF16)

    scatter_hop("E", 0)
    scatter_hop("O", 0)
    scatter_hop("E", 1)
    scatter_hop("O", 1)
    scatter_hop("E", 2)
    scatter_end("O")
    o_last = []
    for k in (4, 3, 5, 2, 6, 1, 7):
        o_last.append(send(d_ref.at[1, k], fo_ref.at[k - 1], along_z(k)))
    scatter_hop("E", 3)
    scatter_end("E")
    e_last = []
    for k in (2, 1, 3):
        e_last.append(send(d_ref.at[0, k], fe_ref.at[k - 1], along_x(k)))
    for which, (lasts, landing) in enumerate(((e_last, fe_ref), (o_last, fo_ref))):
        value = d_ref[which, 0].astype(F32)
        for copy in lasts:
            copy.wait_recv()
        for k in range(len(lasts)):
            value += landing[k].astype(F32)
        fsum_ref[which] = value
    zsend[...] = fsum_ref[1 - yh].astype(BF16)
    zcopy = send(zsend, zrecv, other_half)
    zcopy.wait_recv()
    total = fsum_ref[yh] + zrecv[...].astype(F32)
    out_ref[...] = (stream_ref[...] + unfold(total)).astype(BF16)

    for copy in copies:
        copy.wait_send()


COPIES = 1 + 15 + 7 + 3 + 14 + 6 + 8 * len(GROUPS) + 14 + 6 + 7 + 3 + 1


def per_device(
    queries,
    key_cache,
    value_cache,
    new_key,
    new_value,
    lengths,
    residual,
    norm_gain,
    w_gate,
    w_down,
):
    vmem = pl.BlockSpec(memory_space=pltpu.VMEM)
    smem = pl.BlockSpec(memory_space=pltpu.SMEM)
    hbm = pl.BlockSpec(memory_space=pl.ANY)
    block = (2 * ROWS, HALF)
    most = max(group_rows(group) for group in GROUPS)
    return pl.pallas_call(
        kernel,
        out_shape=jax.ShapeDtypeStruct((ROWS, WIDTH), BF16),
        in_specs=[vmem, hbm, hbm, vmem, vmem, smem, vmem, vmem, hbm, hbm],
        out_specs=vmem,
        scratch_shapes=[
            pltpu.VMEM((ROWS, CACHE, HD), BF16),
            pltpu.VMEM((ROWS, CACHE, HD), BF16),
            pltpu.VMEM((WIDTH, HIDDEN), BF16),
            pltpu.VMEM((HIDDEN, WIDTH), BF16),
            pltpu.VMEM((2, 8, ROWS, HD), F32),
            pltpu.VMEM(block, BF16),
            pltpu.VMEM(block, BF16),
            pltpu.VMEM((ROWS, WIDTH), F32),
            pltpu.VMEM((2, NZ * NX) + block, BF16),
            pltpu.VMEM((most, WIDTH), BF16),
            pltpu.VMEM((2, 256, HIDDEN), F32),
            pltpu.VMEM((256, HIDDEN), BF16),
            pltpu.VMEM((256, HIDDEN), BF16),
            pltpu.VMEM((NY, 256, QUARTER), F32),
            pltpu.VMEM((NY, 256, QUARTER), BF16),
            pltpu.VMEM((NY - 1, 256, QUARTER), BF16),
            pltpu.VMEM((2, NY, 256, QUARTER), BF16),
            pltpu.VMEM((2, NZ * NX) + block, BF16),
            pltpu.VMEM((14, NX // 2) + block, BF16),
            pltpu.VMEM((6, NZ // 2) + block, BF16),
            pltpu.VMEM((NX - 1,) + block, BF16),
            pltpu.VMEM((NZ - 1,) + block, BF16),
            pltpu.VMEM((2,) + block, F32),
            pltpu.VMEM(block, BF16),
            pltpu.VMEM(block, BF16),
            pltpu.SemaphoreType.DMA((4,)),
            pltpu.SemaphoreType.DMA((COPIES,)),
            pltpu.SemaphoreType.DMA((COPIES,)),
        ],
        compiler_params=pltpu.CompilerParams(
            collective_id=0, has_side_effects=True, vmem_limit_bytes=60 * 1024 * 1024
        ),
        cost_estimate=pl.CostEstimate(
            flops=2 * 2 * 512 * WIDTH * HIDDEN, bytes_accessed=6 * 2**20, transcendentals=0
        ),
    )(
        queries,
        key_cache,
        value_cache,
        new_key,
        new_value,
        lengths,
        residual,
        norm_gain.reshape(1, WIDTH),
        w_gate,
        w_down,
    )


def solution(mesh):
    rows = ("req", "ffn")
    return jax.shard_map(
        per_device,
        mesh=mesh,
        in_specs=(
            P(rows, "head"),
            P(rows, None, "head"),
            P(rows, None, "head"),
            P(rows, "head"),
            P(rows, "head"),
            P(rows),
            P(rows, "head"),
            P("head"),
            P("head", rows),
            P(rows, "head"),
        ),
        out_specs=P(rows, "head"),
        check_vma=False,
    )
```

time: 710 us -> 94.4 us (0.13)
  the two profiles are of different devices: /device:TPU:8 before, /device:TPU:2 now
where the time goes in v1:
time: 94.4 us; the launch traced here: 94.1 us
  Pallas kernels  91.4 us (97%)
  local copies, waits for them, and re-layouts  2.67 us (3%)
    pallas_call x1, Pallas kernels, per_device(): pl.pallas_call(kernel, out_shape=jax.ShapeDtypeStruct((ROWS, WIDTH), BF16...  91.4 us

profile of v1, /device:TPU:2, one launch (start us, length us, event | category | flops | bytes accessed | tf_op | source)
XLA Modules:
  0.0 94.1 jit_solution(15491436566121925392)
XLA Ops:
  0.0 1.3 %reshape.3.gain_ref = bf16[1,2048]{1,0:T(2,128)(2,1)} reshape(bf16[2048]{0:T(1024)(128)(2,1)} %param.17) | data formatting | bytes 8192 | tf_op jit(solution)/shard_map/reshape | solution.py:526
  1.3 91.4 %shard_map.100 = bf16[8,2048]{1,0:T(8,128)(2,1)} custom-call(bf16[8,2048]{1,0:T(8,128)(2,1)} %q_ref.1, bf16[8,256,128]{2,1,0:T(8,128)(2,1)} %k_hbm.1, bf16[8,256,128]{2,1,0:T(8,128)(2,1)} %v_hbm.1, bf16[8,128]{1,0:T(8,128)(2,1)} %nk_ref.1, bf16[8,128]{1,0:T(8,128)(2,1)} %nv_ref.1, s32[8]{0:T(128)} %len_ref.1, bf16[8,2048]{1,0:T(8,128)(2,1)} %res_ref.1, ...), custom_call_target="tpu_custom_call" | custom-call | flops 2147483648 | bytes 6291456 | tf_op jit(solution)/shard_map/pallas_call | solution.py:477
  92.7 1.4 %copy.12 = bf16[8,2048]{1,0:T(8,128)(2,1)} copy(bf16[8,2048]{1,0:T(8,128)(2,1)} %shard_map.100) | data formatting | bytes 65536

commit v2 on v1

--- a/solution.py
+++ b/solution.py
@@ -31,6 +31,7 @@
 )
 FLOW = {"E": 0, "O": 1}
 BLOCKS = {"E": NX, "O": NZ}
+Z_ORDER = (0, 4, 3, 5, 2, 6, 1, 7)
 
 
 def group_rows(group):
@@ -41,12 +42,13 @@
     return sum(group_rows(group) for group in GROUPS[:g]) // 2
 
 
-RING_ORDER = (("p", 0), ("m", 1), ("p", 1), ("m", 0))
+FAR = (("p", 0), ("m", 1))
+NEAR = (("p", 1), ("m", 0))
+RING_ORDER = FAR + NEAR
 
 
 def hops_of(n, direction, half):
-    far = 0 if direction == "p" else 1
-    return n // 2 if half == far else n // 2 - 1
+    return n // 2 if (direction, half) in FAR else n // 2 - 1
 
 
 def fold(wide):
@@ -91,7 +93,6 @@
     ro_ref,
     fe_ref,
     fo_ref,
-    fsum_ref,
     zsend,
     zrecv,
     load_sem,
@@ -201,15 +202,17 @@
 
     pl.semaphore_wait(barrier, len(peers))
 
+    def send_squares(dh):
+        return [
+            send(sq_ref.at[0, 0], sq_ref.at[dh, (8 - dk) % 8], same_rows(dh, dk))
+            for dk in range(8)
+            if dh or dk
+        ]
+
+    sq_own = send_squares(0)
     ycopy = send(ysend, yrecv, other_half)
-    sq_copies = []
-    for dh in range(2):
-        for dk in range(8):
-            if dh or dk:
-                sq_copies.append(
-                    send(sq_ref.at[0, 0], sq_ref.at[dh, (8 - dk) % 8], same_rows(dh, dk))
-                )
-    gain = gain_ref[...].astype(F32)
+    sq_other = send_squares(1)
+    gain = gain_ref[...].astype(F32).reshape(1, WIDTH)
 
     def normed(rows, dh):
         total = sq_ref[dh, 0]
@@ -218,18 +221,30 @@
         inverse = lax.rsqrt(jnp.sum(total, axis=1, keepdims=True) / D + EPSILON)
         return fold(rows * inverse * gain).astype(BF16)
 
-    for copy in sq_copies:
-        copy.wait_recv()
-    x_ref[yh, 0] = normed(stream, 0)
-    ycopy.wait_recv()
-    x_ref[1 - yh, 0] = normed(unfold(yrecv[...].astype(F32)), 1)
-
-    o_first = []
-    for k in (4, 3, 5, 2, 6, 1, 7):
-        o_first.append(send(x_ref.at[1, 0], x_ref.at[1, NZ - k], along_z(k)))
-    e_first = []
-    for k in (2, 1, 3):
-        e_first.append(send(x_ref.at[0, 0], x_ref.at[0, NX - k], along_x(k)))
+    o_first, e_first = {}, {}
+
+    def first_sends(kind):
+        if kind == "O":
+            for copy in sq_own:
+                copy.wait_recv()
+            x_ref[1, 0] = normed(stream_ref[...], 0)
+            for slot in range(1, NZ):
+                o_first[slot] = send(
+                    x_ref.at[1, 0], x_ref.at[1, slot], along_z(-Z_ORDER[slot])
+                )
+        else:
+            for copy in sq_other:
+                copy.wait_recv()
+            ycopy.wait_recv()
+            x_ref[0, 0] = normed(unfold(yrecv[...].astype(F32)), 1)
+            for slot in (1, 2, 3):
+                e_first[slot] = send(x_ref.at[0, 0], x_ref.at[0, slot], along_x(-slot))
+
+    def first_end(kind, half):
+        blocks = BLOCKS[kind] // 2
+        for slot in range(half * blocks, (half + 1) * blocks):
+            if slot:
+                (e_first if kind == "E" else o_first)[slot].wait_recv()
 
     rings = {"E": (NZ, along_z), "O": (NX, along_x)}
 
@@ -237,21 +252,32 @@
         blocks = BLOCKS[kind] // 2
         return ref.at[FLOW[kind], pl.ds(slot * BLOCKS[kind] + half * blocks, blocks)]
 
-    arriving = {}
-
-    def gather_hop(kind, s):
+    arriving, skipping = {}, {}
+
+    def gather_end():
+        for copy in skipping.values():
+            copy.wait_recv()
+
+    def gather_hop(kind, s, which=RING_ORDER):
         n, along = rings[kind]
-        for direction, half in RING_ORDER:
+        for direction, half in which:
             if (kind, direction, half, s - 1) in arriving:
                 arriving[kind, direction, half, s - 1].wait_recv()
-            if s >= hops_of(n, direction, half):
-                continue
             step = 1 if direction == "p" else -1
-            arriving[kind, direction, half, s] = send(
-                chunk(x_ref, kind, (-step * s) % n, half),
-                chunk(x_ref, kind, (-step * (s + 1)) % n, half),
-                along(step),
-            )
+            hops = hops_of(n, direction, half)
+            skip = kind == "E" and hops == n // 2
+            if s < hops - skip:
+                arriving[kind, direction, half, s] = send(
+                    chunk(x_ref, kind, (-step * s) % n, half),
+                    chunk(x_ref, kind, (-step * (s + 1)) % n, half),
+                    along(step),
+                )
+            if skip and s == hops - 2:
+                skipping[direction] = send(
+                    chunk(x_ref, kind, (-step * s) % n, half),
+                    chunk(x_ref, kind, (-step * (s + 2)) % n, half),
+                    along(2 * step),
+                )
 
     step_copies = {}
 
@@ -339,46 +365,6 @@
                 d_ref[FLOW[kind], slot * n : (slot + 1) * n, :, columns] = both[row : row + n]
                 row += n
 
-    for copy in e_first:
-        copy.wait_recv()
-    gather_hop("E", 0)
-    for copy in o_first:
-        copy.wait_recv()
-    gather_hop("O", 0)
-    loads[2].wait()
-    gate(0)
-    gather_hop("E", 1)
-    gate(1)
-    reduce_y(0)
-    gather_hop("O", 1)
-    gather_hop("E", 2)
-    activate(0)
-    gate(2)
-    reduce_y(1)
-    gather_hop("E", 3)
-    activate(1)
-    share_core(0)
-    gate(3)
-    reduce_y(2)
-    activate(2)
-    share_core(1)
-    gather_hop("E", 4)
-    gather_hop("O", 2)
-    gate(4)
-    reduce_y(3)
-    loads[3].wait()
-    down(0)
-    reduce_y(4)
-    activate(3)
-    share_core(2)
-    down(1)
-    activate(4)
-    share_core(3)
-    down(2)
-    share_core(4)
-    down(3)
-    down(4)
-
     recv_at = {"E": {}, "O": {}}
     for kind in ("E", "O"):
         n, _ = rings[kind]
@@ -390,64 +376,125 @@
     recv_refs = {"E": re_ref, "O": ro_ref}
     sums = {}
 
-    def scatter_hop(kind, s):
+    def scatter_hop(kind, s, which=RING_ORDER):
         n, along = rings[kind]
         landing = recv_refs[kind]
         blocks = BLOCKS[kind] // 2
-        for direction, half in RING_ORDER:
-            hops, t = hops_of(n, direction, half), s
-            if t >= hops:
-                continue
+        for direction, half in which:
+            hops = hops_of(n, direction, half)
             step = 1 if direction == "p" else -1
-            slot = (step * (hops - t)) % n
-            if t > 0:
-                sums[kind, direction, half, t - 1].wait_recv()
-                first = slot * BLOCKS[kind] + half * blocks
-                own = d_ref[FLOW[kind], first : first + blocks].astype(F32)
-                came = landing[recv_at[kind][direction, half, t - 1]].astype(F32)
-                d_ref[FLOW[kind], first : first + blocks] = (own + came).astype(BF16)
-            sums[kind, direction, half, t] = send(
+            slot = (step * (hops - s)) % n
+            skip = kind == "E" and hops == n // 2
+            came = [s - 1] if s > 0 else []
+            if skip:
+                came = {0: [], 1: [], 2: [0, 1], 3: [2]}[s]
+            first = slot * BLOCKS[kind] + half * blocks
+            if came:
+                value = d_ref[FLOW[kind], first : first + blocks].astype(F32)
+                for t in came:
+                    sums[kind, direction, half, t].wait_recv()
+                    value += landing[recv_at[kind][direction, half, t]].astype(F32)
+                d_ref[FLOW[kind], first : first + blocks] = value.astype(BF16)
+            sums[kind, direction, half, s] = send(
                 chunk(d_ref, kind, slot, half),
-                landing.at[recv_at[kind][direction, half, t]],
-                along(step),
+                landing.at[recv_at[kind][direction, half, s]],
+                along(2 * step if skip and s == 0 else step),
             )
 
-    def scatter_end(kind):
+    def scatter_end(kind, half):
         n, _ = rings[kind]
         blocks = BLOCKS[kind] // 2
-        for half in range(2):
-            value = d_ref[FLOW[kind], half * blocks : (half + 1) * blocks].astype(F32)
-            for direction in ("p", "m"):
-                last = hops_of(n, direction, half) - 1
-                sums[kind, direction, half, last].wait_recv()
-                value += recv_refs[kind][recv_at[kind][direction, half, last]].astype(F32)
-            d_ref[FLOW[kind], half * blocks : (half + 1) * blocks] = value.astype(BF16)
-
-    scatter_hop("E", 0)
-    scatter_hop("O", 0)
-    scatter_hop("E", 1)
-    scatter_hop("O", 1)
-    scatter_hop("E", 2)
-    scatter_end("O")
-    o_last = []
-    for k in (4, 3, 5, 2, 6, 1, 7):
-        o_last.append(send(d_ref.at[1, k], fo_ref.at[k - 1], along_z(k)))
-    scatter_hop("E", 3)
-    scatter_end("E")
-    e_last = []
-    for k in (2, 1, 3):
-        e_last.append(send(d_ref.at[0, k], fe_ref.at[k - 1], along_x(k)))
-    for which, (lasts, landing) in enumerate(((e_last, fe_ref), (o_last, fo_ref))):
-        value = d_ref[which, 0].astype(F32)
-        for copy in lasts:
+        value = d_ref[FLOW[kind], half * blocks : (half + 1) * blocks].astype(F32)
+        for direction in ("p", "m"):
+            last = hops_of(n, direction, half) - 1
+            sums[kind, direction, half, last].wait_recv()
+            value += recv_refs[kind][recv_at[kind][direction, half, last]].astype(F32)
+        d_ref[FLOW[kind], half * blocks : (half + 1) * blocks] = value.astype(BF16)
+        for slot in range(half * blocks, (half + 1) * blocks):
+            if slot == 0:
+                continue
+            if kind == "O":
+                last_copies[kind].append(
+                    send(d_ref.at[1, slot], fo_ref.at[slot - 1], along_z(Z_ORDER[slot]))
+                )
+            else:
+                last_copies[kind].append(
+                    send(d_ref.at[0, slot], fe_ref.at[slot - 1], along_x(slot))
+                )
+
+    last_copies = {"E": [], "O": []}
+
+    def last_end(kind):
+        landing = fe_ref if kind == "E" else fo_ref
+        value = d_ref[FLOW[kind], 0].astype(F32)
+        for copy in last_copies[kind]:
             copy.wait_recv()
-        for k in range(len(lasts)):
+        for k in range(BLOCKS[kind] - 1):
             value += landing[k].astype(F32)
-        fsum_ref[which] = value
-    zsend[...] = fsum_ref[1 - yh].astype(BF16)
+        return value
+
+    first_sends("O")
+    first_sends("E")
+    first_end("E", 0)
+    gather_hop("E", 0, (("p", 0), ("m", 0)))
+    first_end("E", 1)
+    gather_hop("E", 0, (("m", 1), ("p", 1)))
+    first_end("O", 0)
+    gather_hop("O", 0, (("p", 0), ("m", 0)))
+    first_end("O", 1)
+    gather_hop("O", 0, (("m", 1), ("p", 1)))
+    loads[2].wait()
+    gather_hop("E", 1)
+    gate(0)
+    gate(1)
+    reduce_y(0)
+    reduce_y(1)
+    gather_hop("E", 2)
+    gather_hop("O", 1)
+    gate(2)
+    reduce_y(2)
+    gather_hop("E", 3)
+    gate(3)
+    activate(0)
+    activate(1)
+    reduce_y(3)
+    gather_end()
+    gather_hop("O", 2)
+    gate(4)
+    loads[3].wait()
+    reduce_y(4)
+    activate(2)
+    activate(3)
+    share_core(0)
+    share_core(1)
+    down(0)
+    down(1)
+    activate(4)
+    share_core(2)
+    down(2)
+    share_core(3)
+    down(3)
+    share_core(4)
+    down(4)
+    scatter_hop("E", 0, FAR)
+    scatter_hop("E", 1, FAR)
+    scatter_hop("O", 0, FAR)
+    scatter_hop("E", 0, NEAR)
+    scatter_hop("O", 0, NEAR)
+    scatter_hop("E", 2, FAR)
+    scatter_hop("E", 1, NEAR)
+    scatter_hop("O", 1, FAR)
+    scatter_hop("E", 3, FAR)
+    scatter_hop("E", 2, NEAR)
+    scatter_end("O", 0)
+    scatter_end("O", 1)
+    scatter_end("E", 0)
+    scatter_end("E", 1)
+    zsend[...] = last_end("E").astype(BF16)
     zcopy = send(zsend, zrecv, other_half)
+    total = last_end("O")
     zcopy.wait_recv()
-    total = fsum_ref[yh] + zrecv[...].astype(F32)
+    total += zrecv[...].astype(F32)
     out_ref[...] = (stream_ref[...] + unfold(total)).astype(BF16)
 
     for copy in copies:
@@ -502,7 +549,6 @@
             pltpu.VMEM((6, NZ // 2) + block, BF16),
             pltpu.VMEM((NX - 1,) + block, BF16),
             pltpu.VMEM((NZ - 1,) + block, BF16),
-            pltpu.VMEM((2,) + block, F32),
             pltpu.VMEM(block, BF16),
             pltpu.VMEM(block, BF16),
             pltpu.SemaphoreType.DMA((4,)),
@@ -523,7 +569,7 @@
         new_value,
         lengths,
         residual,
-        norm_gain.reshape(1, WIDTH),
+        norm_gain,
         w_gate,
         w_down,
     )

time: 94.4 us -> 84.8 us (0.90)
  the two profiles are of different devices: /device:TPU:2 before, /device:TPU:8 now
where the time goes in v2:
time: 84.8 us; the launch traced here: 84.5 us
  Pallas kernels  83.1 us (98%)
  local copies, waits for them, and re-layouts  1.38 us (2%)
    pallas_call x1, Pallas kernels, per_device(): pl.pallas_call(kernel, out_shape=jax.ShapeDtypeStruct((ROWS, WIDTH), BF16...  83.1 us

profile of v2, /device:TPU:8, one launch (start us, length us, event | category | flops | bytes accessed | tf_op | source)
XLA Modules:
  0.0 84.5 jit_solution(5922434629457633545)
XLA Ops:
  0.0 83.1 %shard_map.100 = bf16[8,2048]{1,0:T(8,128)(2,1)} custom-call(bf16[8,2048]{1,0:T(8,128)(2,1)} %q_ref.1, bf16[8,256,128]{2,1,0:T(8,128)(2,1)} %k_hbm.1, bf16[8,256,128]{2,1,0:T(8,128)(2,1)} %v_hbm.1, bf16[8,128]{1,0:T(8,128)(2,1)} %nk_ref.1, bf16[8,128]{1,0:T(8,128)(2,1)} %nv_ref.1, s32[8]{0:T(128)} %len_ref.1, bf16[8,2048]{1,0:T(8,128)(2,1)} %res_ref.1, ...), custom_call_target="tpu_custom_call" | custom-call | flops 2147483648 | bytes 6291456 | tf_op jit(solution)/shard_map/pallas_call | solution.py:524
  83.1 1.4 %copy.12 = bf16[8,2048]{1,0:T(8,128)(2,1)} copy(bf16[8,2048]{1,0:T(8,128)(2,1)} %shard_map.100) | data formatting | bytes 65536

commit v3 on v2

--- a/solution.py
+++ b/solution.py
@@ -45,6 +45,7 @@
 FAR = (("p", 0), ("m", 1))
 NEAR = (("p", 1), ("m", 0))
 RING_ORDER = FAR + NEAR
+FAR_LINKS = {"E": 2, "O": 1}
 
 
 def hops_of(n, direction, half):
@@ -60,17 +61,22 @@
 
 
 def kernel(
-    q_ref,
+    q_hbm,
     k_hbm,
     v_hbm,
-    nk_ref,
-    nv_ref,
+    nk_hbm,
+    nv_hbm,
     len_ref,
-    res_ref,
-    gain_ref,
+    res_hbm,
+    gain_hbm,
     wg_hbm,
     wd_hbm,
     out_ref,
+    q_ref,
+    nk_ref,
+    nv_ref,
+    res_ref,
+    gain_ref,
     k_ref,
     v_ref,
     wg_ref,
@@ -122,7 +128,17 @@
 
     loads = []
     for i, (src, dst) in enumerate(
-        ((k_hbm, k_ref), (v_hbm, v_ref), (wg_hbm, wg_ref), (wd_hbm, wd_ref))
+        (
+            (q_hbm, q_ref),
+            (nk_hbm, nk_ref),
+            (k_hbm, k_ref),
+            (v_hbm, v_ref),
+            (nv_hbm, nv_ref),
+            (res_hbm, res_ref),
+            (gain_hbm, gain_ref),
+            (wg_hbm, wg_ref),
+            (wd_hbm, wd_ref),
+        )
     ):
         copy = pltpu.make_async_copy(src, dst, load_sem.at[i])
         copy.start()
@@ -151,6 +167,8 @@
         copies.append(copy)
         return copy
 
+    for i in (0, 1, 4, 5, 6):
+        loads[i].wait()
     q = q_ref[...].astype(F32)
     q_all = jnp.concatenate([q[:, HD * j : HD * (j + 1)] for j in range(HEADS)], axis=0)
     request = lax.broadcasted_iota(jnp.int32, (HEADS * ROWS, 1), 0) % ROWS
@@ -161,7 +179,7 @@
     new_key = jnp.concatenate([nk_ref[...].astype(F32)] * HEADS, axis=0)
     new_value = jnp.concatenate([nv_ref[...].astype(F32)] * HEADS, axis=0)
     self_score = jnp.sum(q_all * new_key, axis=1, keepdims=True) * scale
-    loads[0].wait()
+    loads[2].wait()
     scores = jnp.zeros((HEADS * ROWS, CACHE), F32)
     for r in range(ROWS):
         scores += lax.dot_general(
@@ -180,7 +198,7 @@
     totals = jnp.sum(raised, axis=1, keepdims=True) + self_raised
     weights = raised / totals
     self_weight = (self_raised / totals).astype(BF16).astype(F32)
-    loads[1].wait()
+    loads[3].wait()
     blended = self_weight * new_value
     for r in range(ROWS):
         blended += jnp.dot(
@@ -384,21 +402,21 @@
             hops = hops_of(n, direction, half)
             step = 1 if direction == "p" else -1
             slot = (step * (hops - s)) % n
-            skip = kind == "E" and hops == n // 2
-            came = [s - 1] if s > 0 else []
-            if skip:
-                came = {0: [], 1: [], 2: [0, 1], 3: [2]}[s]
+            links = FAR_LINKS[kind] if hops == n // 2 else 1
+            joined = {e: [e - 1] for e in range(1 if links == 1 else 2, hops + 1)}
+            if links > 1:
+                joined[links] = [0] + joined[links]
             first = slot * BLOCKS[kind] + half * blocks
-            if came:
+            if s in joined:
                 value = d_ref[FLOW[kind], first : first + blocks].astype(F32)
-                for t in came:
+                for t in joined[s]:
                     sums[kind, direction, half, t].wait_recv()
                     value += landing[recv_at[kind][direction, half, t]].astype(F32)
                 d_ref[FLOW[kind], first : first + blocks] = value.astype(BF16)
             sums[kind, direction, half, s] = send(
                 chunk(d_ref, kind, slot, half),
                 landing.at[recv_at[kind][direction, half, s]],
-                along(2 * step if skip and s == 0 else step),
+                along(links * step if s == 0 else step),
             )
 
     def scatter_end(kind, half):
@@ -406,9 +424,11 @@
         blocks = BLOCKS[kind] // 2
         value = d_ref[FLOW[kind], half * blocks : (half + 1) * blocks].astype(F32)
         for direction in ("p", "m"):
-            last = hops_of(n, direction, half) - 1
-            sums[kind, direction, half, last].wait_recv()
-            value += recv_refs[kind][recv_at[kind][direction, half, last]].astype(F32)
+            hops = hops_of(n, direction, half)
+            direct = [0] if hops == n // 2 == FAR_LINKS[kind] > 1 else []
+            for t in direct + [hops - 1]:
+                sums[kind, direction, half, t].wait_recv()
+                value += recv_refs[kind][recv_at[kind][direction, half, t]].astype(F32)
         d_ref[FLOW[kind], half * blocks : (half + 1) * blocks] = value.astype(BF16)
         for slot in range(half * blocks, (half + 1) * blocks):
             if slot == 0:
@@ -443,7 +463,7 @@
     gather_hop("O", 0, (("p", 0), ("m", 0)))
     first_end("O", 1)
     gather_hop("O", 0, (("m", 1), ("p", 1)))
-    loads[2].wait()
+    loads[7].wait()
     gather_hop("E", 1)
     gate(0)
     gate(1)
@@ -461,7 +481,7 @@
     gather_end()
     gather_hop("O", 2)
     gate(4)
-    loads[3].wait()
+    loads[8].wait()
     reduce_y(4)
     activate(2)
     activate(3)
@@ -472,15 +492,15 @@
     activate(4)
     share_core(2)
     down(2)
+    scatter_hop("O", 0, NEAR)
     share_core(3)
     down(3)
+    scatter_hop("E", 1, FAR)
+    scatter_hop("E", 0, NEAR)
     share_core(4)
     down(4)
+    scatter_hop("O", 0, FAR)
     scatter_hop("E", 0, FAR)
-    scatter_hop("E", 1, FAR)
-    scatter_hop("O", 0, FAR)
-    scatter_hop("E", 0, NEAR)
-    scatter_hop("O", 0, NEAR)
     scatter_hop("E", 2, FAR)
     scatter_hop("E", 1, NEAR)
     scatter_hop("O", 1, FAR)
@@ -524,9 +544,14 @@
     return pl.pallas_call(
         kernel,
         out_shape=jax.ShapeDtypeStruct((ROWS, WIDTH), BF16),
-        in_specs=[vmem, hbm, hbm, vmem, vmem, smem, vmem, vmem, hbm, hbm],
+        in_specs=[hbm, hbm, hbm, hbm, hbm, smem, hbm, hbm, hbm, hbm],
         out_specs=vmem,
         scratch_shapes=[
+            pltpu.VMEM((ROWS, WIDTH), BF16),
+            pltpu.VMEM((ROWS, HD), BF16),
+            pltpu.VMEM((ROWS, HD), BF16),
+            pltpu.VMEM((ROWS, WIDTH), BF16),
+            pltpu.VMEM((WIDTH,), BF16),
             pltpu.VMEM((ROWS, CACHE, HD), BF16),
             pltpu.VMEM((ROWS, CACHE, HD), BF16),
             pltpu.VMEM((WIDTH, HIDDEN), BF16),
@@ -551,7 +576,7 @@
             pltpu.VMEM((NZ - 1,) + block, BF16),
             pltpu.VMEM(block, BF16),
             pltpu.VMEM(block, BF16),
-            pltpu.SemaphoreType.DMA((4,)),
+            pltpu.SemaphoreType.DMA((9,)),
             pltpu.SemaphoreType.DMA((COPIES,)),
             pltpu.SemaphoreType.DMA((COPIES,)),
         ],

time: 84.8 us -> 83.4 us (0.983)
  the two profiles are of different devices: /device:TPU:8 before, /device:TPU:16 now
where the time goes in v3:
time: 83.4 us; the launch traced here: 83.2 us
  Pallas kernels  81.8 us (98%)
  local copies, waits for them, and re-layouts  1.38 us (2%)
    pallas_call x1, Pallas kernels, per_device(): pl.pallas_call(kernel, out_shape=jax.ShapeDtypeStruct((ROWS, WIDTH), BF16...  81.8 us

profile of v3, /device:TPU:16, one launch (start us, length us, event | category | flops | bytes accessed | tf_op | source)
XLA Modules:
  0.0 83.2 jit_solution(848047003464379844)
XLA Ops:
  0.0 81.8 %shard_map.100 = bf16[8,2048]{1,0:T(8,128)(2,1)} custom-call(bf16[8,2048]{1,0:T(8,128)(2,1)} %q_hbm.1, bf16[8,256,128]{2,1,0:T(8,128)(2,1)} %k_hbm.1, bf16[8,256,128]{2,1,0:T(8,128)(2,1)} %v_hbm.1, bf16[8,128]{1,0:T(8,128)(2,1)} %nk_hbm.1, bf16[8,128]{1,0:T(8,128)(2,1)} %nv_hbm.1, s32[8]{0:T(128)} %len_ref.1, bf16[8,2048]{1,0:T(8,128)(2,1)} %res_hbm.1, ...), custom_call_target="tpu_custom_call" | custom-call | flops 2147483648 | bytes 6291456 | tf_op jit(solution)/shard_map/pallas_call | solution.py:544
  81.8 1.4 %copy.12 = bf16[8,2048]{1,0:T(8,128)(2,1)} copy(bf16[8,2048]{1,0:T(8,128)(2,1)} %shard_map.100) | data formatting | bytes 65536
